TPU v7x, 128 devices: a whole 4x4x4 slice. The times are simulated.
128 devices in a mesh: seq: 16 (over y, x_lo, core), tensor: 8 (over z, x_hi).
Axes of the slice: x: 4 (x_hi: 2, x_lo: 2; x = x_hi * 2 + x_lo), y: 4, z: 4, core: 2. Of those that a mesh axis runs over, the one named last changes fastest.
Arguments:
- tokens: bfloat16 [2048, 16384], P('seq', 'tensor'), may hold values from -100 to 100
- norm_gain: float32 [16384], P('tensor'), may hold values from 0.5 to 1.5
- projection_weight: bfloat16 [2048, 16384], P('tensor', 'seq'), may hold values from -1.5 to 1.5
- panel_index: int32 [1], replicated, may hold values from 0 to 31
Outputs:
- gram: float32 [16384, 16384], P('seq', 'tensor')
- factor_panel: bfloat16 [16384, 512], P('seq')
- projected: float32 [2048, 512], P('tensor', 'seq')
All inputs are finite; a program needn't handle non-finite values.
Results may differ from a plain program's by a relative error of at most 0.0057.
Values may be sent and summed in bfloat16 or wider, within the bound.
A program may use at most 128 MiB of HBM per device.

v0:
```python
import jax
import jax.numpy as jnp
from jax import lax
from jax.sharding import PartitionSpec as P

D = 16384
PANEL = 512
epsilon = 1e-05
damping = 0.1


def broadcast(value, axis, source):
    kept = jnp.where(lax.axis_index(axis) == source, value, 0).astype(value.dtype)
    return lax.psum(kept, axis)


def on_device(tokens, norm_gain, projection_weight, panel_index):
    token_values = tokens.astype(jnp.float32)
    squares = lax.psum(jnp.sum(token_values * token_values, axis=1), "tensor")
    scaled = token_values * lax.rsqrt(squares / D + epsilon)[:, None] * norm_gain[None, :]
    normed = scaled.astype(jnp.bfloat16)
    column_width = normed.shape[1]
    row_width = column_width * lax.axis_size("tensor") // lax.axis_size("seq")
    blocks = column_width // row_width
    seq_index = lax.axis_index("seq")
    tensor_index = lax.axis_index("tensor")
    columns = lax.all_gather(normed, "seq", axis=0, tiled=True)
    local_rows = lax.dynamic_slice_in_dim(columns, seq_index % blocks * row_width, row_width, 1)
    row_part = broadcast(local_rows, "tensor", seq_index // blocks)
    tokens_all = columns.shape[0]
    gram_tile = (
        lax.dot_general(
            row_part, columns, (((0,), (0,)), ((), ())), preferred_element_type=jnp.float32
        )
        / tokens_all
    )
    normed_wide = normed.astype(jnp.float32)
    trace_sum = lax.psum(jnp.sum(normed_wide * normed_wide), ("seq", "tensor")) / tokens_all
    diag_shift = damping * trace_sum / D
    row_ids = seq_index * row_width + lax.iota(jnp.int32, row_width)
    col_ids = tensor_index * column_width + lax.iota(jnp.int32, column_width)
    shifted = gram_tile + jnp.where(
        row_ids[:, None] == col_ids[None, :], diag_shift, jnp.float32(0.0)
    )
    panel_start = panel_index[0] * PANEL
    owner_column = panel_start // column_width
    offset = panel_start - owner_column * column_width
    panel_rows = lax.dynamic_slice_in_dim(shifted, offset, PANEL, 1)
    piece_rows = min(PANEL, row_width)
    global_row = panel_start + 0
    source = global_row // row_width
    local_offset = global_row - source * row_width
    piece = lax.dynamic_slice_in_dim(panel_rows, local_offset, piece_rows, 0)
    pieces = broadcast(piece, "seq", source)
    diag_block = pieces
    identity = jnp.eye(PANEL, dtype=jnp.float32)
    diag_block = jnp.where(tensor_index == owner_column, diag_block, identity)
    factor = jnp.linalg.cholesky(diag_block)
    solved = lax.linalg.triangular_solve(
        factor, panel_rows, left_side=False, lower=True, transpose_a=True
    )
    whitened_rows = solved.astype(jnp.bfloat16)
    whitened_full = broadcast(whitened_rows, "tensor", owner_column)
    partial_value = jnp.dot(projection_weight, whitened_full, preferred_element_type=jnp.float32)
    projected = lax.psum_scatter(partial_value, "seq", scatter_dimension=1, tiled=True)
    return (shifted, whitened_full, projected)


def solution(mesh):
    placed = (P("seq", "tensor"), P("tensor"), P("tensor", "seq"), P())
    return jax.shard_map(
        on_device,
        mesh=mesh,
        in_specs=placed,
        out_specs=(P("seq", "tensor"), P("seq", None), P("tensor", "seq")),
        check_vma=False,
    )
```

profile of v0, /device:TPU:0, one launch (start us, length us, event | category | flops | bytes accessed | tf_op | source)
XLA Modules:
  0.0 742.1 jit_solution(978973545675533625)
XLA Ops:
  8.5 25.6 %psum.35 = f32[128]{0:T(128)S(1)} all-reduce(f32[128]{0:T(128)S(1)} %fusion.9), channel_id=1, replica_groups=mesh['seq'=16,'tensor'=8] {'tensor'}, use_global_device_ids=true, to_apply=%region_1.0 | all-reduce | flops 128 | bytes 1024 | tf_op jit(solution)/shard_map/psum | solution.py:19
  34.1 2.7 multiply_reduce_fusion
  36.9 48.6 %all-gather.2.cloned.1.call-done = bf16[2048,2048]{1,0:T(8,128)(2,1)} async-done(((bf16[128,2048]{1,0:T(8,128)(2,1)}), bf16[2048,2048]{1,0:T(8,128)(2,1)}) %all-gather.2.cloned.1.call-update) | async-done | bytes 8388624 | tf_op jit(solution)/shard_map/all_gather | solution.py:27
  85.5 5.4 dynamic-slice_select_fusion
  91.0 209.9 %psum.37 = f32[]{:T(128)} all-reduce(f32[]{:T(128)} %get-tuple-element.26), channel_id=1, replica_groups=mesh['seq'=16,'tensor'=8] {'seq','tensor'}, use_global_device_ids=true, to_apply=%region_4.5 | all-reduce | flops 1 | bytes 8 | tf_op jit(solution)/shard_map/psum | solution.py:38
  302.3 13.0 %select_add_fusion = f32[1024,2048]{0,1:T(8,128)S(1)} fusion(bf16[2048,1024]{1,0:T(8,128)(2,1)} %all-reduce.5.cloned.1.call-done, bf16[2048,2048]{1,0:T(8,128)(2,1)} %all-gather.2.cloned.1.call-done, f32[]{:T(128)S(6)} %div.53, s32[1024]{0:T(1024)S(1)} %iota_add_fusion.1, s32[2048]{0:T(1024)S(1)} %iota_add_fusion), kind=kOutput, calls=%fused_computation.2 | convolution fusion | flops 8598323200 | bytes 20983812 | tf_op jit(solution)/shard_map/dot_general | solution.py:32
  315.4 3.2 copy-done.1
  318.6 1.3 dynamic-slice_select_fusion.1
  320.5 116.3 %all-reduce.7.cloned.1.call-done = f32[512,512]{0,1:T(8,128)} async-done(((f32[512,512]{0,1:T(8,128)}), f32[512,512]{0,1:T(8,128)}) %all-reduce.7.cloned.1.call-update) | async-done | bytes 1048592 | tf_op jit(solution)/shard_map/psum | solution.py:14
  438.2 1.5 fusion.15
  439.7 11.7 %cholesky.103 = f32[128,128]{1,0:T(8,128)S(1)} custom-call(f32[128,128]{1,0:T(8,128)S(1)} %cholesky.263), custom_call_target="Cholesky" | custom-call | tf_op jit(solution)/shard_map/jit(cholesky)/cholesky | solution.py:58
  451.4 9.8 %custom-call.30 = f32[1,128,128]{1,2,0:T(8,128)S(1)} custom-call(f32[1,128,128]{2,1,0:T(8,128)S(1)} %get-tuple-element.35), custom_call_target="InvertDiagBlocksLowerTriangular" | custom-call | tf_op jit(solution)/shard_map/jit(cholesky)/cholesky | solution.py:58
  461.9 11.7 %cholesky.215 = f32[128,128]{1,0:T(8,128)S(1)} custom-call(f32[128,128]{1,0:T(8,128)S(1)} %cholesky.267), custom_call_target="Cholesky" | custom-call | tf_op jit(solution)/shard_map/jit(cholesky)/cholesky | solution.py:58
  474.0 9.9 %custom-call.31 = f32[1,128,128]{1,2,0:T(8,128)S(1)} custom-call(f32[1,128,128]{2,1,0:T(8,128)S(1)} %get-tuple-element.33), custom_call_target="InvertDiagBlocksLowerTriangular" | custom-call | tf_op jit(solution)/shard_map/jit(cholesky)/cholesky | solution.py:58
  485.0 11.7 %cholesky.236 = f32[128,128]{1,0:T(8,128)S(1)} custom-call(f32[128,128]{1,0:T(8,128)S(1)} %cholesky.272), custom_call_target="Cholesky" | custom-call | tf_op jit(solution)/shard_map/jit(cholesky)/cholesky | solution.py:58
  496.9 9.8 %custom-call.32 = f32[1,128,128]{1,2,0:T(8,128)S(1)} custom-call(f32[1,128,128]{2,1,0:T(8,128)S(1)} %get-tuple-element.31), custom_call_target="InvertDiagBlocksLowerTriangular" | custom-call | tf_op jit(solution)/shard_map/jit(cholesky)/cholesky | solution.py:58
  507.5 11.9 %cholesky.253 = f32[128,128]{1,0:T(8,128)S(1)} custom-call(f32[128,128]{1,0:T(8,128)S(1)} %convolution_subtract_fusion.4), custom_call_target="Cholesky" | custom-call | tf_op jit(solution)/shard_map/jit(cholesky)/cholesky | solution.py:58
  524.1 8.5 %while.1 = (s32[]{:T(128)}, f32[512,512]{0,1:T(8,128)S(1)}, s32[4,2]{0,1:T(2,128)S(1)}, f32[4,128,128]{2,1,0:T(8,128)S(1)}, s32[]{:T(128)}) while((s32[]{:T(128)}, f32[512,512]{0,1:T(8,128)S(1)}, s32[4,2]{0,1:T(2,128)S(1)}, f32[4,128,128]{2,1,0:T(8,128)S(1)}, s32[]{:T(128)}) %tuple.33), condition=%wide.while_cond, body=%wide.while_body.sunk | while | flops 2 | bytes 393321 | solution.py:59
  524.7 1.4 dynamic-slice.18
  526.8 1.4 dynamic-slice.18
  528.9 1.4 dynamic-slice.18
  531.1 1.4 dynamic-slice.18
  532.6 39.3 %custom-call.33 = f32[4,128,128]{1,2,0:T(8,128)S(1)} custom-call(f32[4,128,128]{2,1,0:T(8,128)S(1)} %get-tuple-element.10), custom_call_target="InvertDiagBlocksLowerTriangular" | custom-call | tf_op jit(solution)/shard_map/triangular_solve | solution.py:59
  571.9 1.7 fusion.41
  573.6 1.7 convolution_subtract_fusion.1
  575.8 1.8 convolution_subtract_fusion
  578.3 2.2 fusion.6
  582.4 91.5 %all-reduce.9.cloned.1.call-done = bf16[1024,512]{0,1:T(8,128)(2,1)} async-done(((bf16[1024,512]{0,1:T(8,128)(2,1)}), bf16[1024,512]{0,1:T(8,128)(2,1)}) %all-reduce.9.cloned.1.call-update) | async-done | bytes 1048592 | tf_op jit(solution)/shard_map/psum | solution.py:14
  673.9 2.5 convolution_bitcast_fusion
  676.5 9.2 %copy.17 = f32[1024,2048]{1,0:T(8,128)} copy(f32[1024,2048]{0,1:T(8,128)} %copy-done.1) | data formatting | bytes 16777216
  685.7 1.3 copy.18
  687.0 48.4 %reduce-scatter.2.cloned.1.call-done = f32[256,32]{0,1:T(8,128)} async-done(((f32[256,512]{0,1:T(8,128)}), f32[256,32]{0,1:T(8,128)}) %reduce-scatter.2.cloned.1.call-update) | async-done | bytes 32784 | tf_op jit(solution)/shard_map/reduce_scatter | solution.py:65
  (74 shorter events, 14.5 us)
Async XLA Ops:
  7.2 666.8 %copy-start = (bf16[256,1024]{1,0:T(8,128)(2,1)S(1)}, bf16[256,1024]{1,0:T(8,128)(2,1)}, u32[]{:S(2)}) copy-start(bf16[256,1024]{1,0:T(8,128)(2,1)} %param.6) | copy-start | bytes 1572868
  7.2 78.4 %all-gather.2.cloned.1.call-start = ((), (), s32[]{:S(2)}) async-start(), calls=%async_computation.1 | async-start | bytes 8912896 | tf_op jit(solution)/shard_map/all_gather | solution.py:27
  36.8 265.5 %all-reduce.5.cloned.1.call-start = ((), (), s32[]{:S(2)}) async-start(), calls=%async_computation.2 | async-start | bytes 8388608 | tf_op jit(solution)/shard_map/psum | solution.py:14
  91.0 345.8 %all-reduce.7.cloned.1.call-start = ((), (), s32[]{:S(2)}) async-start(), calls=%async_computation.3 | async-start | bytes 2097152 | tf_op jit(solution)/shard_map/psum | solution.py:14
  315.4 3.2 copy-start.1
  319.9 354.0 %all-reduce.9.cloned.1.call-start = ((), (), s32[]{:S(2)}) async-start(), calls=%async_computation.4 | async-start | bytes 2097152 | tf_op jit(solution)/shard_map/psum | solution.py:14
  436.8 1.4 copy-start.2
  582.3 153.0 %reduce-scatter.2.cloned.1.call-start = ((), (), s32[]{:S(2)}) async-start(), calls=%async_computation.5 | async-start | bytes 557056 | tf_op jit(solution)/shard_map/reduce_scatter | solution.py:65
  676.5 9.2 %copy-start.3 = (bf16[1024,512]{0,1:T(8,128)(2,1)S(1)}, bf16[1024,512]{0,1:T(8,128)(2,1)}, u32[]{:S(2)}) copy-start(bf16[1024,512]{0,1:T(8,128)(2,1)} %all-reduce.9.cloned.1.call-done) | copy-start | bytes 3145732
Sparse Core Ops, SparseCore 0:
  36.9 48.5 all-gather.1
  91.1 186.8 all-reduce.4
  320.1 116.6 all-reduce.6
  582.5 91.4 all-reduce.8
  676.8 58.4 reduce-scatter.1
where the time goes:
time: 749 us; the launch traced here: 742 us
  waiting for transfers between devices  305 us (41%)
  blocking collectives  235 us (31%)
  other arithmetic  132 us (18%)
  matrix products  27.1 us (4%)
  local copies, waits for them, and re-layouts  24.1 us (3%)
  between operations  18.2 us (2%)
    psum x1, blocking collectives, on_device(): lax.psum(jnp.sum(normed_wide * normed_wide), ('seq', 'tensor')) / tokens_all  210 us
    psum x3, waiting for transfers between devices, broadcast(): return lax.psum(kept, axis)  208 us
    another operation x14, other arithmetic, on_device(): factor = jnp.linalg.cholesky(diag_block)  78.6 us
    all_gather x1, waiting for transfers between devices, on_device(): columns = lax.all_gather(normed, 'seq', axis=0, tiled=True)  48.6 us
    reduce_scatter x1, waiting for transfers between devices, on_device(): lax.psum_scatter(partial_value, 'seq', scatter_dimension=1, tiled=True)  48.4 us
    another operation x3, other arithmetic, on_device(): lax.linalg.triangular_solve(factor, panel_rows, left_side=False, lower=Tr...  39.4 us
    psum x1, blocking collectives, on_device(): squares = lax.psum(jnp.sum(token_values * token_values, axis=1), 'tensor')  25.6 us
  transfers between devices with their start and end apart: 5, of which 4 were waited for; matrix products, arithmetic and copies ran while one was open for 1% of the time, Pallas kernels for 0%

commit v1 on v0

--- a/solution.py
+++ b/solution.py
@@ -24,7 +24,9 @@
     blocks = column_width // row_width
     seq_index = lax.axis_index("seq")
     tensor_index = lax.axis_index("tensor")
-    columns = lax.all_gather(normed, "seq", axis=0, tiled=True)
+    columns = jnp.concatenate(
+        lax.all_to_all(jnp.stack([normed] * lax.axis_size("seq")), "seq", 0, 0), axis=0
+    )
     local_rows = lax.dynamic_slice_in_dim(columns, seq_index % blocks * row_width, row_width, 1)
     row_part = broadcast(local_rows, "tensor", seq_index // blocks)
     tokens_all = columns.shape[0]

time: 749 us -> 781 us (1.043)
  waiting for transfers between devices: 305 us -> 355 us
  blocking collectives: 235 us -> 209 us
    all_to_all x0 -> x1, waiting for transfers between devices: none -> 95.2 us  [on_device(): lax.all_to_all(jnp.stack([normed] * lax.axis_size('seq')), 'seq', 0, 0)]
    all_gather x1 -> x0, waiting for transfers between devices: 48.6 us -> none  [on_device(): columns = lax.all_gather(normed, 'seq', axis=0, tiled=True)]
    psum x1, blocking collectives: 210 us -> 183 us  [on_device(): lax.psum(jnp.sum(normed_wide * normed_wide), ('seq', 'tensor')) / tokens_all]
where the time goes in v1:
time: 781 us; the launch traced here: 774 us
  waiting for transfers between devices  355 us (45%)
  blocking collectives  209 us (27%)
  other arithmetic  130 us (17%)
  matrix products  28.8 us (4%)
  local copies, waits for them, and re-layouts  27.6 us (4%)
  between operations  18.2 us (2%)
    psum x3, waiting for transfers between devices, broadcast(): return lax.psum(kept, axis)  212 us
    psum x1, blocking collectives, on_device(): lax.psum(jnp.sum(normed_wide * normed_wide), ('seq', 'tensor')) / tokens_all  183 us
    all_to_all x1, waiting for transfers between devices, on_device(): lax.all_to_all(jnp.stack([normed] * lax.axis_size('seq')), 'seq', 0, 0)  95.2 us
    another operation x14, other arithmetic, on_device(): factor = jnp.linalg.cholesky(diag_block)  78.6 us
    reduce_scatter x1, waiting for transfers between devices, on_device(): lax.psum_scatter(partial_value, 'seq', scatter_dimension=1, tiled=True)  48.4 us
    another operation x3, other arithmetic, on_device(): lax.linalg.triangular_solve(factor, panel_rows, left_side=False, lower=Tr...  39.4 us
    psum x1, blocking collectives, on_device(): squares = lax.psum(jnp.sum(token_values * token_values, axis=1), 'tensor')  25.6 us
  transfers between devices with their start and end apart: 5, of which 4 were waited for; matrix products, arithmetic and copies ran while one was open for 1% of the time, Pallas kernels for 0%

profile of v1, /device:TPU:0, one launch (start us, length us, event | category | flops | bytes accessed | tf_op | source)
XLA Modules:
  0.0 773.8 jit_solution(15622555472383051919)
XLA Ops:
  8.5 25.6 %psum.35 = f32[128]{0:T(128)S(1)} all-reduce(f32[128]{0:T(128)S(1)} %fusion.9), channel_id=1, replica_groups=mesh['seq'=16,'tensor'=8] {'tensor'}, use_global_device_ids=true, to_apply=%region_1.0 | all-reduce | flops 128 | bytes 1024 | tf_op jit(solution)/shard_map/psum | solution.py:19
  34.1 2.1 multiply_reduce_fusion
  36.2 4.5 stack.2
  40.7 4.7 all-to-all-start
  45.5 95.2 %all-to-all-done = bf16[16,128,2048]{2,1,0:T(8,128)(2,1)} async-done(((bf16[16,128,2048]{2,1,0:T(8,128)(2,1)}), bf16[16,128,2048]{2,1,0:T(8,128)(2,1)}, u32[]{:S(2)}, u32[]{:S(2)}) %all-to-all-start) | async-done | bytes 8388640 | tf_op jit(solution)/shard_map/all_to_all | solution.py:28
  140.7 5.4 dynamic-slice_select_fusion
  146.2 182.9 %psum.37 = f32[]{:T(128)} all-reduce(f32[]{:T(128)} %get-tuple-element.26), channel_id=1, replica_groups=mesh['seq'=16,'tensor'=8] {'seq','tensor'}, use_global_device_ids=true, to_apply=%region_4.5 | all-reduce | flops 1 | bytes 8 | tf_op jit(solution)/shard_map/psum | solution.py:40
  330.5 13.0 %select_add_fusion = f32[1024,2048]{0,1:T(8,128)S(1)} fusion(bf16[2048,1024]{1,0:T(8,128)(2,1)} %all-reduce.5.cloned.1.call-done, bf16[2048,2048]{1,0:T(8,128)(2,1)} %bitcast, f32[]{:T(128)S(6)} %div.53, s32[1024]{0:T(1024)S(1)} %iota_add_fusion.1, s32[2048]{0:T(1024)S(1)} %iota_add_fusion), kind=kOutput, calls=%fused_computation.2 | convolution fusion | flops 8598323200 | bytes 20983812 | tf_op jit(solution)/shard_map/dot_general | solution.py:34
  343.6 3.2 copy-done.1
  348.7 119.1 %all-reduce.7.cloned.1.call-done = f32[512,512]{0,1:T(8,128)} async-done(((f32[512,512]{0,1:T(8,128)}), f32[512,512]{0,1:T(8,128)}) %all-reduce.7.cloned.1.call-update) | async-done | bytes 1048592 | tf_op jit(solution)/shard_map/psum | solution.py:14
  468.5 11.7 %cholesky.103 = f32[128,128]{1,0:T(8,128)S(1)} custom-call(f32[128,128]{1,0:T(8,128)S(1)} %cholesky.263), custom_call_target="Cholesky" | custom-call | tf_op jit(solution)/shard_map/jit(cholesky)/cholesky | solution.py:60
  480.3 9.8 %custom-call.30 = f32[1,128,128]{1,2,0:T(8,128)S(1)} custom-call(f32[1,128,128]{2,1,0:T(8,128)S(1)} %get-tuple-element.35), custom_call_target="InvertDiagBlocksLowerTriangular" | custom-call | tf_op jit(solution)/shard_map/jit(cholesky)/cholesky | solution.py:60
  490.8 11.7 %cholesky.215 = f32[128,128]{1,0:T(8,128)S(1)} custom-call(f32[128,128]{1,0:T(8,128)S(1)} %cholesky.267), custom_call_target="Cholesky" | custom-call | tf_op jit(solution)/shard_map/jit(cholesky)/cholesky | solution.py:60
  502.8 9.9 %custom-call.31 = f32[1,128,128]{1,2,0:T(8,128)S(1)} custom-call(f32[1,128,128]{2,1,0:T(8,128)S(1)} %get-tuple-element.33), custom_call_target="InvertDiagBlocksLowerTriangular" | custom-call | tf_op jit(solution)/shard_map/jit(cholesky)/cholesky | solution.py:60
  513.3 1.5 convolution_subtract_fusion.3
  514.8 11.7 %cholesky.236 = f32[128,128]{1,0:T(8,128)S(1)} custom-call(f32[128,128]{1,0:T(8,128)S(1)} %cholesky.272), custom_call_target="Cholesky" | custom-call | tf_op jit(solution)/shard_map/jit(cholesky)/cholesky | solution.py:60
  526.7 9.8 %custom-call.32 = f32[1,128,128]{1,2,0:T(8,128)S(1)} custom-call(f32[1,128,128]{2,1,0:T(8,128)S(1)} %get-tuple-element.31), custom_call_target="InvertDiagBlocksLowerTriangular" | custom-call | tf_op jit(solution)/shard_map/jit(cholesky)/cholesky | solution.py:60
  538.1 11.9 %cholesky.253 = f32[128,128]{1,0:T(8,128)S(1)} custom-call(f32[128,128]{1,0:T(8,128)S(1)} %convolution_subtract_fusion.4), custom_call_target="Cholesky" | custom-call | tf_op jit(solution)/shard_map/jit(cholesky)/cholesky | solution.py:60
  554.7 8.5 %while.1 = (s32[]{:T(128)}, f32[512,512]{0,1:T(8,128)S(1)}, s32[4,2]{0,1:T(2,128)S(1)}, f32[4,128,128]{2,1,0:T(8,128)S(1)}, s32[]{:T(128)}) while((s32[]{:T(128)}, f32[512,512]{0,1:T(8,128)S(1)}, s32[4,2]{0,1:T(2,128)S(1)}, f32[4,128,128]{2,1,0:T(8,128)S(1)}, s32[]{:T(128)}) %tuple.33), condition=%wide.while_cond, body=%wide.while_body.sunk | while | flops 2 | bytes 393321 | solution.py:61
  555.3 1.4 dynamic-slice.18
  557.4 1.4 dynamic-slice.18
  559.6 1.4 dynamic-slice.18
  561.7 1.4 dynamic-slice.18
  563.2 39.3 %custom-call.33 = f32[4,128,128]{1,2,0:T(8,128)S(1)} custom-call(f32[4,128,128]{2,1,0:T(8,128)S(1)} %get-tuple-element.10), custom_call_target="InvertDiagBlocksLowerTriangular" | custom-call | tf_op jit(solution)/shard_map/triangular_solve | solution.py:61
  602.5 1.7 fusion.41
  604.2 1.7 convolution_subtract_fusion.1
  606.5 1.8 convolution_subtract_fusion
  608.9 2.2 fusion.6
  613.0 92.6 %all-reduce.9.cloned.1.call-done = bf16[1024,512]{0,1:T(8,128)(2,1)} async-done(((bf16[1024,512]{0,1:T(8,128)(2,1)}), bf16[1024,512]{0,1:T(8,128)(2,1)}) %all-reduce.9.cloned.1.call-update) | async-done | bytes 1048592 | tf_op jit(solution)/shard_map/psum | solution.py:14
  705.6 2.5 convolution_bitcast_fusion
  708.1 9.2 %copy.17 = f32[1024,2048]{1,0:T(8,128)} copy(f32[1024,2048]{0,1:T(8,128)} %copy-done.1) | data formatting | bytes 16777216
  718.6 48.4 %reduce-scatter.2.cloned.1.call-done = f32[256,32]{0,1:T(8,128)} async-done(((f32[256,512]{0,1:T(8,128)}), f32[256,32]{0,1:T(8,128)}) %reduce-scatter.2.cloned.1.call-update) | async-done | bytes 32784 | tf_op jit(solution)/shard_map/reduce_scatter | solution.py:67
  (74 shorter events, 16.6 us)
Async XLA Ops:
  7.2 698.4 %copy-start = (bf16[256,1024]{1,0:T(8,128)(2,1)S(1)}, bf16[256,1024]{1,0:T(8,128)(2,1)}, u32[]{:S(2)}) copy-start(bf16[256,1024]{1,0:T(8,128)(2,1)} %param.6) | copy-start | bytes 1572868
  40.7 100.1 %all-to-all-start = ((bf16[16,128,2048]{2,1,0:T(8,128)(2,1)}), bf16[16,128,2048]{2,1,0:T(8,128)(2,1)}, u32[]{:S(2)}, u32[]{:S(2)}) async-start(bf16[16,128,2048]{2,1,0:T(8,128)(2,1)} %stack.2), calls=%async_computation | async-start | bytes 16777216 | tf_op jit(solution)/shard_map/all_to_all | solution.py:28
  45.4 285.1 %all-reduce.5.cloned.1.call-start = ((), (), s32[]{:S(2)}) async-start(), calls=%async_computation.2 | async-start | bytes 8388608 | tf_op jit(solution)/shard_map/psum | solution.py:14
  146.2 321.6 %all-reduce.7.cloned.1.call-start = ((), (), s32[]{:S(2)}) async-start(), calls=%async_computation.3 | async-start | bytes 2097152 | tf_op jit(solution)/shard_map/psum | solution.py:14
  343.6 3.2 copy-start.1
  348.2 357.4 %all-reduce.9.cloned.1.call-start = ((), (), s32[]{:S(2)}) async-start(), calls=%async_computation.4 | async-start | bytes 2097152 | tf_op jit(solution)/shard_map/psum | solution.py:14
  468.5 34.4 %copy-start.3 = (f32[512,512]{1,0:T(8,128)}, f32[512,512]{1,0:T(8,128)S(1)}, u32[]{:S(2)}) copy-start(f32[512,512]{1,0:T(8,128)S(1)} %fusion.15) | copy-start | bytes 3145732
  613.0 154.0 %reduce-scatter.2.cloned.1.call-start = ((), (), s32[]{:S(2)}) async-start(), calls=%async_computation.5 | async-start | bytes 557056 | tf_op jit(solution)/shard_map/reduce_scatter | solution.py:67
  708.1 9.2 %copy-start.2 = (bf16[1024,512]{0,1:T(8,128)(2,1)S(1)}, bf16[1024,512]{0,1:T(8,128)(2,1)}, u32[]{:S(2)}) copy-start(bf16[1024,512]{0,1:T(8,128)(2,1)} %all-reduce.9.cloned.1.call-done) | copy-start | bytes 3145732
Sparse Core Ops, SparseCore 0:
  146.3 181.6 all-reduce.4
  348.3 119.4 all-reduce.6
  613.1 92.4 all-reduce.8
  708.5 58.4 reduce-scatter.1
